TPU v7x, 256 devices: a whole 4x4x8 slice. The times are simulated.
256 devices in a mesh: depth: 16 (over x_lo, y, core), dp: 16 (over x_hi, z).
Axes of the slice: x: 4 (x_hi: 2, x_lo: 2; x = x_hi * 2 + x_lo), y: 4, z: 8, core: 2. Of those that a mesh axis runs over, the one named last changes fastest.
Arguments:
- token_ids: int32 [2048], P('dp'), may hold values from 0 to 20479
- embedding: bfloat16 [20480, 512], P('depth'), may hold values from -6 to 6
- w_up: bfloat16 [32, 512, 2048], P('depth'), may hold values from -0.25 to 0.25
- w_down: bfloat16 [32, 2048, 512], P('depth'), may hold values from -0.125 to 0.125
- cotangent: bfloat16 [2048, 512], P('dp'), may hold values from -0.119628906 to 0.119628906
Outputs:
- grad_up: float32 [32, 512, 2048], P('depth', 'dp')
- grad_down: float32 [32, 2048, 512], P('depth', 'dp')
All inputs are finite; a program needn't handle non-finite values.
Results may differ from a plain program's by a relative error of at most 0.03.
Values may be sent and summed in bfloat16 or wider, within the bound.
A program may use at most 64 MiB of HBM per device.

v0:
```python
import jax
import jax.numpy as jnp
from jax import lax
from jax.sharding import PartitionSpec as P

RELAX = 3
EPSILON = 1e-06
GAMMA = 0.05


def shifted(block, axis, distance):
    devices = range(lax.axis_size(axis))
    route = [(i - distance, i) for i in devices if i - distance in devices]
    return lax.ppermute(block, axis, route)


def layer_forward(state, weight_up, weight_down):
    scale = lax.rsqrt(jnp.mean(state * state, axis=-1, keepdims=True) + EPSILON)
    normed = (state * scale).astype(jnp.bfloat16)
    before = jnp.dot(normed, weight_up, preferred_element_type=jnp.float32)
    hidden = jax.nn.silu(before).astype(jnp.bfloat16)
    output = state + jnp.dot(hidden, weight_down, preferred_element_type=jnp.float32)
    return (output, (scale, normed, before, hidden))


def layer_adjoint(state, saved, adjoint, weight_up, weight_down):
    scale, normed, before, hidden = saved
    adjoint_low = adjoint.astype(jnp.bfloat16)
    toward_hidden = lax.dot_general(
        adjoint_low, weight_down, (((1,), (1,)), ((), ())), preferred_element_type=jnp.float32
    )
    sigma = jax.nn.sigmoid(before)
    delta = (toward_hidden * sigma * (1.0 + before * (1.0 - sigma))).astype(jnp.bfloat16)
    toward_normed = lax.dot_general(
        delta, weight_up, (((1,), (1,)), ((), ())), preferred_element_type=jnp.float32
    )
    unit = state * scale
    inner = jnp.mean(toward_normed * unit, axis=-1, keepdims=True)
    return (adjoint + scale * (toward_normed - unit * inner), adjoint_low, delta)


def coarse_matrix(weight_up, weight_down):
    total = jnp.dot(weight_up[0], weight_down[0], preferred_element_type=jnp.float32)
    total = total + jnp.dot(weight_up[1], weight_down[1], preferred_element_type=jnp.float32)
    return jnp.eye(weight_up.shape[1], dtype=jnp.float32) + GAMMA * total


def shards(token_ids, embedding, w_up, w_down, cotangent):
    depth = lax.axis_size("depth")
    position = lax.axis_index("depth")
    first = position == 0
    final_block = position == depth - 1
    layers = w_up.shape[0]
    vocab_rows = embedding.shape[0]
    local_ids = token_ids - position * vocab_rows
    inside = (local_ids >= 0) & (local_ids < vocab_rows)
    picked = jnp.take(embedding, jnp.clip(local_ids, 0, vocab_rows - 1), axis=0)
    picked = jnp.where(inside[:, None], picked, jnp.zeros_like(picked)).astype(jnp.float32)
    start = lax.psum(picked.astype(jnp.bfloat16), "depth").astype(jnp.float32)
    matrix = coarse_matrix(w_up, w_down)
    transposed = matrix.T
    zeros = jnp.zeros_like(start)
    coarse = start
    arrived_projection = zeros
    for sweep in range(RELAX):
        run_state = coarse
        for run_layer in range(layers):
            run_state, unused = layer_forward(run_state, w_up[run_layer], w_down[run_layer])
        projection = jnp.dot(coarse, matrix, precision=lax.Precision.HIGHEST)
        arrived, arrived_projection = shifted((run_state, projection), "depth", 1)
        coarse = jnp.where(first, start, arrived)
    tau = coarse - arrived_projection

    def forward_turn(turn, incoming):
        carried = jnp.dot(incoming + tau, matrix, precision=lax.Precision.HIGHEST)
        return shifted(carried.astype(jnp.bfloat16), "depth", 1).astype(carried.dtype)

    incoming = lax.fori_loop(0, depth - 1, forward_turn, zeros)
    corrected = incoming + tau
    states = []
    saves = []
    state = corrected
    for layer in range(layers):
        states.append(state)
        state, saved = layer_forward(state, w_up[layer], w_down[layer])
        saves.append(saved)

    def run_adjoint(adjoint):
        for layer in reversed(range(layers)):
            adjoint, low, delta = layer_adjoint(
                states[layer], saves[layer], adjoint, w_up[layer], w_down[layer]
            )
        return adjoint

    final = cotangent.astype(jnp.float32)
    adjoint_state = final
    back_projection = zeros
    for sweep in range(RELAX):
        begun = run_adjoint(adjoint_state)
        projection = jnp.dot(adjoint_state, transposed, precision=lax.Precision.HIGHEST)
        arrived, back_projection = (
            shifted(begun.astype(jnp.bfloat16), "depth", -1).astype(begun.dtype),
            shifted(projection.astype(jnp.bfloat16), "depth", -1).astype(projection.dtype),
        )
        adjoint_state = jnp.where(final_block, final, arrived)
    back_tau = adjoint_state - back_projection

    def backward_turn(turn, incoming):
        carried = jnp.dot(incoming + back_tau, transposed, precision=lax.Precision.HIGHEST)
        return shifted(carried.astype(jnp.bfloat16), "depth", -1).astype(carried.dtype)

    back_incoming = lax.fori_loop(0, depth - 1, backward_turn, zeros)
    adjoint = back_incoming + back_tau
    lows = [None] * layers
    deltas = [None] * layers
    for layer in reversed(range(layers)):
        adjoint, low, delta = layer_adjoint(
            states[layer], saves[layer], adjoint, w_up[layer], w_down[layer]
        )
        lows[layer] = low
        deltas[layer] = delta
    local_up = jnp.stack(
        [
            lax.dot_general(
                saves[layer][1],
                deltas[layer],
                (((0,), (0,)), ((), ())),
                preferred_element_type=jnp.float32,
            )
            for layer in range(layers)
        ],
        0,
    )
    local_down = jnp.stack(
        [
            lax.dot_general(
                saves[layer][3],
                lows[layer],
                (((0,), (0,)), ((), ())),
                preferred_element_type=jnp.float32,
            )
            for layer in range(layers)
        ],
        0,
    )
    grad_up, grad_down = (
        lax.psum_scatter(
            local_up.astype(jnp.bfloat16), "dp", scatter_dimension=1, tiled=True
        ).astype(jnp.float32),
        lax.psum_scatter(
            local_down.astype(jnp.bfloat16), "dp", scatter_dimension=1, tiled=True
        ).astype(jnp.float32),
    )
    return (grad_up, grad_down)


def solution(mesh):
    in_specs = (
        P("dp"),
        P("depth", None),
        P("depth", None, None),
        P("depth", None, None),
        P("dp", None),
    )
    out_specs = (P("depth", "dp", None), P("depth", "dp", None))
    return jax.shard_map(shards, mesh=mesh, in_specs=in_specs, out_specs=out_specs, check_vma=False)
```

profile of v0, /device:TPU:8, one launch (start us, length us, event | category | flops | bytes accessed | tf_op | source)
XLA Modules:
  0.0 967.2 jit_solution(8096644310616206722)
XLA Ops:
  10.2 121.4 %all-reduce.2.cloned.1.call-done = bf16[128,512]{1,0:T(8,128)(2,1)} async-done(((bf16[128,512]{1,0:T(8,128)(2,1)}), bf16[128,512]{1,0:T(8,128)(2,1)}) %all-reduce.2.cloned.1.call-update) | async-done | bytes 131088 | tf_op jit(solution)/shard_map/psum | solution.py:59
  140.8 4.5 fusion.30
  184.5 119.6 %while.22 = (s32[]{:T(128)}, f32[128,512]{1,0:T(8,128)S(1)}, f32[128,512]{1,0:T(8,128)S(1)}, f32[512,512]{1,0:T(8,128)S(1)}, s32[]{:T(128)}, /*index=5*/s32[]{:T(128)}) while((s32[]{:T(128)}, f32[128,512]{1,0:T(8,128)S(1)}, f32[128,512]{1,0:T(8,128)S(1)}, f32[512,512]{1,0:T(8,128)S(1)}, s32[]{:T(128)}, /*index=5*/s32[]{:T(128)}) %tuple.59), condition=%wide.region_8.9_spmd.clone, body=%wide.region_7.8_spmd.clone.sunk | while | flops 402915328 | bytes 2621559 | solution.py:78
  241.8 6.2 collective-permute-start
  249.7 7.4 collective-permute-start
  258.9 7.4 collective-permute-start
  268.1 7.4 collective-permute-start
  277.3 7.4 collective-permute-start
  286.4 7.4 collective-permute-start
  295.6 7.4 collective-permute-start
  321.9 6.5 collective-permute-done.6
  339.6 7.2 collective-permute-done.7
  351.1 4.9 multiply_reduce_fusion.1
  369.2 139.0 %while.23 = (s32[]{:T(128)}, f32[128,512]{1,0:T(8,128)S(1)}, f32[128,512]{1,0:T(8,128)S(1)}, f32[512,512]{1,0:T(8,128)S(1)}, s32[]{:T(128)}, /*index=5*/s32[]{:T(128)}) while((s32[]{:T(128)}, f32[128,512]{1,0:T(8,128)S(1)}, f32[128,512]{1,0:T(8,128)S(1)}, f32[512,512]{1,0:T(8,128)S(1)}, s32[]{:T(128)}, ...), condition=%wide.region_18.19_spmd.clone, body=%wide.region_17.18_spmd.clone.sunk | while | flops 402915328 | bytes 2621559 | solution.py:112
  371.9 7.2 collective-permute-done.1
  381.8 6.3 collective-permute-done.1
  390.8 7.2 collective-permute-done.1
  400.7 6.5 collective-permute-done.1
  409.9 6.5 collective-permute-done.1
  419.0 6.5 collective-permute-done.1
  428.2 6.5 collective-permute-done.1
  437.4 6.5 collective-permute-done.1
  446.6 6.5 collective-permute-done.1
  455.8 6.5 collective-permute-done.1
  464.9 6.5 collective-permute-done.1
  474.1 6.5 collective-permute-done.1
  483.3 6.5 collective-permute-done.1
  492.5 6.5 collective-permute-done.1
  501.7 6.5 collective-permute-done.1
  519.6 4.9 fusion.6
  528.4 219.8 %reduce-scatter.5.cloned.1.call-done = bf16[2,128,512]{2,1,0:T(8,128)(2,1)} async-done(((bf16[2,2048,512]{2,1,0:T(8,128)(2,1)}), bf16[2,128,512]{2,1,0:T(8,128)(2,1)}) %reduce-scatter.5.cloned.1.call-update) | async-done | bytes 262160 | tf_op jit(solution)/shard_map/reduce_scatter | solution.py:150
  750.0 208.9 %reduce-scatter.3.cloned.1.call-done = bf16[2,32,2048]{2,1,0:T(8,128)(2,1)} async-done(((bf16[2,512,2048]{2,1,0:T(8,128)(2,1)}), bf16[2,32,2048]{2,1,0:T(8,128)(2,1)}) %reduce-scatter.3.cloned.1.call-update) | async-done | bytes 262160 | tf_op jit(solution)/shard_map/reduce_scatter | solution.py:147
  (210 shorter events, 224.9 us)
Async XLA Ops:
  7.2 124.4 %all-reduce.2.cloned.1.call-start = ((), (), s32[]{:S(2)}) async-start(), calls=%async_computation.2 | async-start | bytes 262144 | tf_op jit(solution)/shard_map/psum | solution.py:59
  10.1 738.1 %reduce-scatter.5.cloned.1.call-start = ((), (), s32[]{:S(2)}) async-start(), calls=%async_computation.4 | async-start | bytes 4456448 | tf_op jit(solution)/shard_map/reduce_scatter | solution.py:150
  138.8 9.2 collective-permute-start.2
  154.9 7.9 collective-permute-start.3
  171.2 8.0 collective-permute-start.4
  175.6 7.9 collective-permute-start.5
  249.7 8.4 collective-permute-start
  258.9 8.4 collective-permute-start
  268.1 8.4 collective-permute-start
  277.3 8.4 collective-permute-start
  286.4 8.4 collective-permute-start
  295.6 8.4 collective-permute-start
  319.9 8.4 collective-permute-start.6
  337.7 9.1 collective-permute-start.7
  357.8 8.5 collective-permute-start.8
  360.9 8.3 collective-permute-start.9
  369.9 9.1 collective-permute-start.1
  379.8 8.3 collective-permute-start.1
  388.9 9.1 collective-permute-start.1
  398.8 8.4 collective-permute-start.1
  408.0 8.4 collective-permute-start.1
  417.1 8.4 collective-permute-start.1
  426.3 8.4 collective-permute-start.1
  435.5 8.4 collective-permute-start.1
  444.7 8.4 collective-permute-start.1
  453.9 8.4 collective-permute-start.1
  463.0 8.4 collective-permute-start.1
  472.2 8.4 collective-permute-start.1
  481.4 8.4 collective-permute-start.1
  490.6 8.4 collective-permute-start.1
  499.7 8.4 collective-permute-start.1
  517.4 441.5 %reduce-scatter.3.cloned.1.call-start = ((), (), s32[]{:S(2)}) async-start(), calls=%async_computation.3 | async-start | bytes 4456448 | tf_op jit(solution)/shard_map/reduce_scatter | solution.py:147
  (24 other events, 195.4 us)
Sparse Core Ops, SparseCore 0:
  11.2 120.3 all-reduce.1
  517.5 230.6 reduce-scatter.4
  752.2 206.5 reduce-scatter.2
where the time goes:
time: 969 us; the launch traced here: 967 us
  waiting for transfers between devices  716 us (74%)
  starting transfers between devices  113 us (12%)
  matrix products  96.1 us (10%)
  other arithmetic  19.6 us (2%)
  between operations  14.2 us (1%)
    reduce_scatter x1, waiting for transfers between devices, shards(): lax.psum_scatter(local_down.astype(jnp.bfloat16), 'dp', scatter_dimension...  220 us
    reduce_scatter x1, waiting for transfers between devices, shards(): lax.psum_scatter(local_up.astype(jnp.bfloat16), 'dp', scatter_dimension=1...  209 us
    ppermute x38, waiting for transfers between devices, shifted(): return lax.ppermute(block, axis, route)  166 us
    psum x1, waiting for transfers between devices, shards(): start = lax.psum(picked.astype(jnp.bfloat16), 'depth').astype(jnp.float32)  121 us
    ppermute x38, starting transfers between devices, shifted(): return lax.ppermute(block, axis, route)  113 us
    dot_general x7, matrix products, layer_adjoint(): lax.dot_general(delta, weight_up, (((1,), (1,)), ((), ())), preferred_ele...  26.2 us
    dot_general x7, matrix products, layer_forward(): jnp.dot(hidden, weight_down, preferred_element_type=jnp.float32)  21.1 us
  transfers between devices with their start and end apart: 41, of which 41 were waited for; matrix products, arithmetic and copies ran while one was open for 3% of the time, Pallas kernels for 0%

commit v1 on v0

--- a/solution.py
+++ b/solution.py
@@ -56,7 +56,9 @@
     inside = (local_ids >= 0) & (local_ids < vocab_rows)
     picked = jnp.take(embedding, jnp.clip(local_ids, 0, vocab_rows - 1), axis=0)
     picked = jnp.where(inside[:, None], picked, jnp.zeros_like(picked)).astype(jnp.float32)
-    start = lax.psum(picked.astype(jnp.bfloat16), "depth").astype(jnp.float32)
+    start = jnp.sum(lax.all_gather(picked.astype(jnp.bfloat16), "depth"), axis=0).astype(
+        jnp.float32
+    )
     matrix = coarse_matrix(w_up, w_down)
     transposed = matrix.T
     zeros = jnp.zeros_like(start)

time: 969 us -> 885 us (0.913)
  waiting for transfers between devices: 716 us -> 633 us
    psum x1 -> x0, waiting for transfers between devices: 121 us -> none  [shards(): start = lax.psum(picked.astype(jnp.bfloat16), 'depth').astype(jnp.float32)]
    all_gather x0 -> x1, waiting for transfers between devices: none -> 39.3 us  [shards(): lax.all_gather(picked.astype(jnp.bfloat16), 'depth')]
where the time goes in v1:
time: 885 us; the launch traced here: 884 us
  waiting for transfers between devices  633 us (72%)
  starting transfers between devices  111 us (13%)
  matrix products  96.1 us (11%)
  other arithmetic  20.6 us (2%)
  between operations  14.2 us (2%)
    reduce_scatter x1, waiting for transfers between devices, shards(): lax.psum_scatter(local_down.astype(jnp.bfloat16), 'dp', scatter_dimension...  220 us
    reduce_scatter x1, waiting for transfers between devices, shards(): lax.psum_scatter(local_up.astype(jnp.bfloat16), 'dp', scatter_dimension=1...  209 us
    ppermute x38, waiting for transfers between devices, shifted(): return lax.ppermute(block, axis, route)  165 us
    ppermute x38, starting transfers between devices, shifted(): return lax.ppermute(block, axis, route)  111 us
    all_gather x1, waiting for transfers between devices, shards(): lax.all_gather(picked.astype(jnp.bfloat16), 'depth')  39.3 us
    dot_general x7, matrix products, layer_adjoint(): lax.dot_general(delta, weight_up, (((1,), (1,)), ((), ())), preferred_ele...  26.2 us
    dot_general x7, matrix products, layer_forward(): jnp.dot(hidden, weight_down, preferred_element_type=jnp.float32)  21.1 us
  transfers between devices with their start and end apart: 41, of which 41 were waited for; matrix products, arithmetic and copies ran while one was open for 3% of the time, Pallas kernels for 0%

profile of v1, /device:TPU:8, one launch (start us, length us, event | category | flops | bytes accessed | tf_op | source)
XLA Modules:
  0.0 883.6 jit_solution(10207585350663441745)
XLA Ops:
  10.2 39.3 %all-gather.2.cloned.1.call-done = bf16[16,128,512]{2,1,0:T(8,128)(2,1)} async-done(((bf16[1,128,512]{2,1,0:T(8,128)(2,1)}), bf16[16,128,512]{2,1,0:T(8,128)(2,1)}) %all-gather.2.cloned.1.call-update) | async-done | bytes 2097168 | tf_op jit(solution)/shard_map/all_gather | solution.py:59
  59.8 4.5 fusion.30
  101.8 118.2 %while.22 = (s32[]{:T(128)}, f32[128,512]{1,0:T(8,128)S(1)}, f32[128,512]{1,0:T(8,128)S(1)}, f32[512,512]{1,0:T(8,128)S(1)}, s32[]{:T(128)}, /*index=5*/s32[]{:T(128)}) while((s32[]{:T(128)}, f32[128,512]{1,0:T(8,128)S(1)}, f32[128,512]{1,0:T(8,128)S(1)}, f32[512,512]{1,0:T(8,128)S(1)}, s32[]{:T(128)}, /*index=5*/s32[]{:T(128)}) %tuple.60), condition=%wide.region_8.9_spmd.clone, body=%wide.region_7.8_spmd.clone.sunk | while | flops 402915328 | bytes 2621559 | solution.py:80
  159.1 4.8 collective-permute-start
  166.2 6.9 collective-permute-start
  174.9 7.4 collective-permute-start
  184.1 7.4 collective-permute-start
  193.3 7.4 collective-permute-start
  202.4 7.4 collective-permute-start
  211.6 7.4 collective-permute-start
  237.8 6.5 collective-permute-done.6
  255.6 7.2 collective-permute-done.7
  267.1 4.9 multiply_reduce_fusion.1
  285.2 139.0 %while.23 = (s32[]{:T(128)}, f32[128,512]{1,0:T(8,128)S(1)}, f32[128,512]{1,0:T(8,128)S(1)}, f32[512,512]{1,0:T(8,128)S(1)}, s32[]{:T(128)}, /*index=5*/s32[]{:T(128)}) while((s32[]{:T(128)}, f32[128,512]{1,0:T(8,128)S(1)}, f32[128,512]{1,0:T(8,128)S(1)}, f32[512,512]{1,0:T(8,128)S(1)}, s32[]{:T(128)}, ...), condition=%wide.region_18.19_spmd.clone, body=%wide.region_17.18_spmd.clone.sunk | while | flops 402915328 | bytes 2621559 | solution.py:114
  287.8 7.2 collective-permute-done.1
  297.7 6.3 collective-permute-done.1
  306.8 7.2 collective-permute-done.1
  316.7 6.5 collective-permute-done.1
  325.9 6.5 collective-permute-done.1
  335.0 6.5 collective-permute-done.1
  344.2 6.5 collective-permute-done.1
  353.4 6.5 collective-permute-done.1
  362.6 6.5 collective-permute-done.1
  371.8 6.5 collective-permute-done.1
  380.9 6.5 collective-permute-done.1
  390.1 6.5 collective-permute-done.1
  399.3 6.5 collective-permute-done.1
  408.5 6.5 collective-permute-done.1
  417.6 6.5 collective-permute-done.1
  435.6 4.9 fusion.6
  444.4 219.7 %reduce-scatter.5.cloned.1.call-done = bf16[2,128,512]{2,1,0:T(8,128)(2,1)} async-done(((bf16[2,2048,512]{2,1,0:T(8,128)(2,1)}), bf16[2,128,512]{2,1,0:T(8,128)(2,1)}) %reduce-scatter.5.cloned.1.call-update) | async-done | bytes 262160 | tf_op jit(solution)/shard_map/reduce_scatter | solution.py:152
  665.9 209.5 %reduce-scatter.3.cloned.1.call-done = bf16[2,32,2048]{2,1,0:T(8,128)(2,1)} async-done(((bf16[2,512,2048]{2,1,0:T(8,128)(2,1)}), bf16[2,32,2048]{2,1,0:T(8,128)(2,1)}) %reduce-scatter.3.cloned.1.call-update) | async-done | bytes 262160 | tf_op jit(solution)/shard_map/reduce_scatter | solution.py:149
  (209 shorter events, 224.8 us)
Async XLA Ops:
  7.2 42.3 %all-gather.2.cloned.1.call-start = ((), (), s32[]{:S(2)}) async-start(), calls=%async_computation.2 | async-start | bytes 2228224 | tf_op jit(solution)/shard_map/all_gather | solution.py:59
  10.1 653.9 %reduce-scatter.5.cloned.1.call-start = ((), (), s32[]{:S(2)}) async-start(), calls=%async_computation.4 | async-start | bytes 4456448 | tf_op jit(solution)/shard_map/reduce_scatter | solution.py:152
  57.7 7.7 collective-permute-start.2
  72.3 7.9 collective-permute-start.3
  88.6 8.0 collective-permute-start.4
  92.9 7.9 collective-permute-start.5
  166.2 7.9 collective-permute-start
  174.9 8.4 collective-permute-start
  184.1 8.4 collective-permute-start
  193.3 8.4 collective-permute-start
  202.4 8.4 collective-permute-start
  211.6 8.4 collective-permute-start
  235.9 8.4 collective-permute-start.6
  253.7 9.1 %collective-permute-start.7 = (bf16[128,512]{1,0:T(8,128)(2,1)S(1)}, bf16[128,512]{1,0:T(8,128)(2,1)S(1)}, u32[]{:S(2)}, u32[]{:S(2)}) collective-permute-start(bf16[128,512]{1,0:T(8,128)(2,1)S(1)} %add_convert_fusion.2), channel_id=1, source_target_pairs={{16,0},{32,16},{48,32},{64,48},{80,64},{96,80},{112,96},{128,112},... | collective-permute-start | bytes 393224 | tf_op jit(solution)/shard_map/ppermute | solution.py:14
  273.8 8.5 collective-permute-start.8
  276.9 8.3 collective-permute-start.9
  285.9 9.1 %collective-permute-start.1 = (bf16[128,512]{1,0:T(8,128)(2,1)S(1)}, bf16[128,512]{1,0:T(8,128)(2,1)S(1)}, u32[]{:S(2)}, u32[]{:S(2)}) collective-permute-start(bf16[128,512]{1,0:T(8,128)(2,1)S(1)} %convolution_convert_fusion.10), channel_id=1, source_target_pairs={{16,0},{32,16},{48,32},{64,48},{80,64},{96,80},{112,96},{128,112},... | collective-permute-start | bytes 393224 | tf_op jit(solution)/shard_map/while/body/eval_jaxpr/ppermute | solution.py:14
  295.8 8.3 collective-permute-start.1
  304.9 9.1 %collective-permute-start.1 = (bf16[128,512]{1,0:T(8,128)(2,1)S(1)}, bf16[128,512]{1,0:T(8,128)(2,1)S(1)}, u32[]{:S(2)}, u32[]{:S(2)}) collective-permute-start(bf16[128,512]{1,0:T(8,128)(2,1)S(1)} %convolution_convert_fusion.10), channel_id=1, source_target_pairs={{16,0},{32,16},{48,32},{64,48},{80,64},{96,80},{112,96},{128,112},... | collective-permute-start | bytes 393224 | tf_op jit(solution)/shard_map/while/body/eval_jaxpr/ppermute | solution.py:14
  314.7 8.4 collective-permute-start.1
  323.9 8.4 collective-permute-start.1
  333.1 8.4 collective-permute-start.1
  342.3 8.4 collective-permute-start.1
  351.5 8.4 collective-permute-start.1
  360.6 8.4 collective-permute-start.1
  369.8 8.4 collective-permute-start.1
  379.0 8.4 collective-permute-start.1
  388.2 8.4 collective-permute-start.1
  397.4 8.4 collective-permute-start.1
  406.5 8.4 collective-permute-start.1
  415.7 8.4 collective-permute-start.1
  433.4 441.9 %reduce-scatter.3.cloned.1.call-start = ((), (), s32[]{:S(2)}) async-start(), calls=%async_computation.3 | async-start | bytes 4456448 | tf_op jit(solution)/shard_map/reduce_scatter | solution.py:149
  (23 other events, 185.2 us)
Sparse Core Ops, SparseCore 0:
  10.4 39.0 all-gather.1
  433.5 230.5 reduce-scatter.4
  668.6 206.6 reduce-scatter.2
